TPU v7x, 512 devices: a whole 4x4x16 slice. The times are simulated.
512 devices in a mesh: src: 16 (over z), tgt: 32 (over x, y, core).
Axes of the slice: x: 4, y: 4, z: 16, core: 2. Of those that a mesh axis runs over, the one named last changes fastest.
Arguments:
- source_embed: bfloat16 [32768, 256], P('src'), may hold values from -0.375 to 0.375
- target_embed: bfloat16 [32768, 256], P('tgt'), may hold values from -0.375 to 0.375
- target_feat: bfloat16 [32768, 128], P('tgt'), may hold values from -6 to 6
- source_mass: float32 [32768], P('src'), may hold values from 0.05 to 20
- target_mass: float32 [32768], P('tgt'), may hold values from 0.05 to 20
Outputs:
- source_potential: float32 [32768], P('src')
- target_potential: float32 [32768], P('tgt')
- projected: float32 [32768, 128], P(('src', 'tgt'))
All inputs are finite; a program needn't handle non-finite values.
Results may differ from a plain program's by a relative error of at most 0.001.
Values sent between devices are 32-bit elements; how exact they have to be, the bound alone decides.
No kernel may reach another device: no remote copies, remote signals or barrier semaphores. Data moves between devices by JAX's collectives and lax.ppermute only.
A program may use at most 192 MiB of HBM per device.

v0:
```python
import functools
import math

import jax
import jax.numpy as jnp
from jax import lax
from jax.experimental import pallas as pl
from jax.experimental.pallas import tpu as pltpu
from jax.sharding import PartitionSpec as P

ENTROPY = 0.05
LANES = 128
WIDTH = 256
ONE_SCALE = 1.0 / ENTROPY * math.log2(math.e)
TWO_SCALE = 2.0 * ONE_SCALE
ONE_UNIT = ENTROPY * math.log(2.0)
LOWEST, HIGHEST = 2.0**-90, 2.0**110
NT = (((1,), (1,)), ((), ()))
NN = (((1,), (0,)), ((), ()))
HALVES = WIDTH // LANES
SLAB = 512
ACCUMULATE = 32
VMEM_LIMIT = 40 * 1024 * 1024


def merge(parts):
    top = jnp.max(parts, axis=0)
    total = jnp.sum(jnp.exp2((parts - top[None]) * ONE_SCALE), axis=0)
    return top + ENTROPY * jnp.log(total)


def lanes_to_rows(values, col_ref):
    for k in range(values.shape[0]):
        square = jnp.broadcast_to(values[k : k + 1, :], (LANES, LANES))
        col_ref[pl.ds(k * LANES, LANES), :] = square.T


def fold(reduce, part):
    return reduce(part.reshape(-1, ACCUMULATE, LANES), axis=0)


def exponents(p_ref, q, col_ref, s, rows=SLAB):
    slab = pl.ds(s * rows, rows)
    cross = lax.dot_general(p_ref[slab, :], q, NT, preferred_element_type=jnp.float32)
    col = col_ref[slab, :]
    return [cross[:, h * LANES : (h + 1) * LANES] * TWO_SCALE + col for h in range(HALVES)]


def scores(p_ref, q, col_ref, z_ref, s, rows=SLAB):
    slab = pl.ds(s * rows, rows)
    tops = []
    for h, part in enumerate(exponents(p_ref, q, col_ref, s, rows)):
        z_ref[slab, pl.ds(h * LANES, LANES)] = part
        tops.append(fold(jnp.max, part))
    return tops


def weigh(z_ref, tops, s, rows=SLAB):
    slab = pl.ds(s * rows, rows)
    weights, totals = [], []
    for h, top in enumerate(tops):
        part = z_ref[slab, pl.ds(h * LANES, LANES)]
        weight = jnp.exp2(part - top)
        weights.append(weight)
        totals.append(fold(jnp.sum, weight))
    return weights, totals


def join(op, held, more):
    return more if held is None else [op(a, b) for a, b in zip(held, more)]


def settle(reduce, values):
    return [reduce(value, axis=0, keepdims=True) for value in values]


def log_sum(top, total):
    return ONE_UNIT * top + ENTROPY * jnp.log(total)


def run_chunks(p_ref, chunk, chunks, col_ref, z_refs, emit, rows=2 * SLAB):
    slabs = p_ref.shape[0] // rows
    tops = None
    for t in range(chunks + 1):
        q = chunk(t) if t < chunks else None
        later, totals, weights = None, None, []
        for s in range(slabs):
            if t < chunks:
                later = join(jnp.maximum, later, scores(p_ref, q, col_ref, z_refs[t % 2], s, rows))
            if t > 0:
                weight, total = weigh(z_refs[(t - 1) % 2], tops, s, rows)
                totals = join(jnp.add, totals, total)
                weights.append(weight)
        if t > 0:
            emit(t - 1, tops, settle(jnp.sum, totals), weights)
        if t < chunks:
            tops = settle(jnp.max, later)


def log_sums(p_ref, q_ref, col_ref, z_ref, row_ref, rows=2 * SLAB):
    slabs, chunks = p_ref.shape[0] // SLAB, q_ref.shape[0] // WIDTH
    totals = [None] * chunks
    for s in range(p_ref.shape[0] // rows):
        for t in range(chunks):
            parts = exponents(p_ref, q_ref[pl.ds(t * WIDTH, WIDTH), :], col_ref, s, rows)
            totals[t] = join(jnp.add, totals[t], [fold(jnp.sum, jnp.exp2(part)) for part in parts])
    for t in range(chunks):
        for h, total in enumerate(settle(jnp.sum, totals[t])):
            row_ref[pl.ds(t * HALVES + h, 1), :] = total
    sums = row_ref[...]
    row_ref[...] = ENTROPY * jnp.log(sums)
    safe = jnp.logical_and(jnp.min(sums) >= LOWEST, jnp.max(sums) <= HIGHEST)

    @pl.when(jnp.logical_not(safe))
    def _():
        @pl.loop(0, chunks)
        def _(t):
            q = q_ref[pl.ds(pl.multiple_of(t * WIDTH, WIDTH), WIDTH), :]
            tops, sums = None, None
            for s in range(slabs):
                tops = join(jnp.maximum, tops, scores(p_ref, q, col_ref, z_ref, s))
            tops = settle(jnp.max, tops)
            for s in range(slabs):
                sums = join(jnp.add, sums, weigh(z_ref, tops, s)[1])
            for h, pair in enumerate(zip(tops, settle(jnp.sum, sums))):
                row_ref[pl.ds(t * HALVES + h, 1), :] = log_sum(*pair)


def first_kernel(
    p_hbm, q_hbm, p_mass_hbm, q_mass_hbm, out_ref, p_ref, q_ref, p_log_ref, q_log_ref,
    p_sems, sems, col_ref, z_ref, row_ref,
):
    loads = []
    for s in range(p_ref.shape[0] // SLAB):
        slab = pl.ds(s * SLAB, SLAB)
        loads.append(pltpu.make_async_copy(p_hbm.at[slab, :], p_ref.at[slab, :], p_sems.at[s]))
    load_q = pltpu.make_async_copy(q_hbm, q_ref, sems.at[0])
    masses = [
        pltpu.make_async_copy(p_mass_hbm, p_log_ref, sems.at[1]),
        pltpu.make_async_copy(q_mass_hbm, q_log_ref, sems.at[2]),
    ]
    for copy in loads + [load_q] + masses:
        copy.start()
    for s, copy in enumerate(loads):
        copy.wait()
        slab = pl.ds(s * SLAB, SLAB)
        p = p_ref[slab, :].astype(jnp.float32)
        norms = jnp.sum(p * p, axis=1, keepdims=True)
        col_ref[slab, :] = jnp.broadcast_to(-ONE_SCALE * norms, (SLAB, LANES))
    load_q.wait()
    log_sums(p_ref, q_ref, col_ref, z_ref, row_ref)
    for copy in masses:
        copy.wait()
    p_log_ref[...] = ENTROPY * jnp.log(p_log_ref[...])
    q_log_ref[...] = ENTROPY * jnp.log(q_log_ref[...])
    out_ref[...] = jnp.broadcast_to(row_ref[...][None], out_ref.shape)


def next_kernel(parts_ref, log_ref, p_ref, q_ref, out_ref, col_ref, z_ref, row_ref):
    lanes_to_rows(ONE_SCALE * (log_ref[...] - merge(parts_ref[...])), col_ref)
    log_sums(p_ref, q_ref, col_ref, z_ref, row_ref)
    out_ref[...] = jnp.broadcast_to(row_ref[...][None], out_ref.shape)


def last_kernel(
    parts_ref, log_ref, p_ref, q_ref, feat_ref,
    sent_ref, keep_ref, own_ref, bias_ref, flip_ref, col_ref, even_ref, odd_ref,
):
    core = lax.rem(lax.axis_index("tgt"), 2)
    chips, _, share, depth = q_ref.shape
    half = chips * share
    width = feat_ref.shape[1]
    blocks = WIDTH // share
    bias = log_ref[...] - merge(parts_ref[...])
    bias_ref[...] = bias
    lanes_to_rows(ONE_SCALE * bias, col_ref)
    flip_ref[...] = feat_ref[...].astype(jnp.float32).T.astype(jnp.bfloat16)
    sent_ref[pl.ds(width, 8), :] = jnp.zeros((8, half), jnp.float32)
    own_ref[...] = jnp.zeros((8, half), jnp.float32)

    def chunk(t):
        own, first = divmod(t * WIDTH, half)
        q = q_ref[pl.ds(first // share, blocks), core if own else 1 - core]
        return q.reshape(WIDTH, depth)

    def emit(t, tops, totals, weights):
        own, first = divmod(t * WIDTH, half)
        slabs = [
            jnp.concatenate([weight.astype(jnp.bfloat16) for weight in slab], axis=1)
            for slab in weights
        ]
        lanes = pl.ds(first, WIDTH)
        lse = jnp.concatenate([log_sum(*pair) for pair in zip(tops, totals)], axis=1)
        scale = 1.0 / jnp.concatenate(totals, axis=1)
        sent_ref[pl.ds(width + own, 1), lanes] = lse
        own_ref[pl.ds(own, 1), lanes] = lse
        if own:
            for s, slab in enumerate(slabs):
                keep_ref[pl.ds(s * slab.shape[0], slab.shape[0]), lanes] = slab
            own_ref[pl.ds(2, 1), lanes] = scale
        else:
            weight = jnp.concatenate(slabs, axis=0)
            numer = lax.dot_general(
                flip_ref[...], weight, NN, preferred_element_type=jnp.float32
            )
            sent_ref[pl.ds(0, width), lanes] = numer * scale

    run_chunks(p_ref, chunk, 2 * half // WIDTH, col_ref, (even_ref, odd_ref), emit)


def squares(ref, k):
    rows = ref[pl.ds(k * LANES, LANES), :].astype(jnp.float32)
    norms = jnp.sum(rows * rows, axis=1, keepdims=True)
    return jnp.broadcast_to(norms, (LANES, LANES)).T[:1, :]


def own_kernel(
    keep_ref, own_ref, flip_ref, bias_ref, p_ref, q_ref, log_ref, mean_ref, pot_ref, base_ref
):
    numer = lax.dot_general(
        flip_ref[...], keep_ref[...], NN, preferred_element_type=jnp.float32
    )
    mean_ref[...] = numer * own_ref[pl.ds(2, 1), :]
    for k in range(pot_ref.shape[0]):
        row = pl.ds(k, 1)
        pot_ref[row, :] = bias_ref[row, :] + squares(p_ref, k)
    for k in range(base_ref.shape[0]):
        row = pl.ds(k, 1)
        base_ref[row, :] = log_ref[row, :] + squares(q_ref, k)


def pair_kernel(far_chip, mean_ref, own_ref, came_ref, out_ref, row_ref):
    width, half = mean_ref.shape
    chips = out_ref.shape[0]
    share = half // chips
    rows = half // LANES
    for side in range(2):
        mine = own_ref[pl.ds(1 - side, 1), :]
        other = came_ref[pl.ds(width + side, 1), :]
        top = jnp.maximum(mine, other)
        mine_share = jnp.exp2((mine - top) * ONE_SCALE)
        other_share = jnp.exp2((other - top) * ONE_SCALE)
        total = mine_share + other_share
        lse = top + ENTROPY * jnp.log(total)
        for k in range(rows):
            row_ref[pl.ds(side * rows + k, 1), :] = lse[:, k * LANES : (k + 1) * LANES]
        if side == 0:
            scale = 1.0 / total
            mine_share, other_share = mine_share * scale, other_share * scale
            step = LANES // share
            for k in range(rows):
                lanes = slice(k * LANES, (k + 1) * LANES)
                block = (
                    mean_ref[:, lanes] * mine_share[:, lanes]
                    + came_ref[pl.ds(0, width), lanes] * other_share[:, lanes]
                )
                place = (k * step - far_chip) % chips
                out_ref[pl.ds(place, step), pl.ds(0, share), :] = block.T.reshape(
                    step, share, LANES
                )
    out_ref[:, pl.ds(share, 2 * rows), :] = jnp.broadcast_to(
        row_ref[...][None], (chips, 2 * rows, LANES)
    )


def final_kernel(landed_ref, base_ref, pot_ref, out_ref):
    index = lax.axis_index("tgt")
    core, chip = lax.rem(index, 2), lax.div(index, 2)
    share = out_ref.shape[0]
    chips = landed_ref.shape[0]
    mine = landed_ref[:, pl.ds(share + lax.div(chip, 2), 1), :].reshape(chips, LANES)
    mine = jnp.exp2((mine - jnp.max(mine, axis=0, keepdims=True)) * ONE_SCALE)
    mine = mine / jnp.sum(mine, axis=0, keepdims=True)
    mine = jnp.where(lax.rem(chip, 2) == 0, mine, pltpu.roll(mine, share, 1))
    mine = jnp.concatenate([mine, jnp.zeros((LANES - chips, LANES), jnp.float32)], axis=0).T
    total = jnp.zeros(out_ref.shape, jnp.float32)
    for b in range(chips):
        scale = jnp.broadcast_to(mine[:share, b : b + 1], out_ref.shape)
        total = total + landed_ref[b, pl.ds(0, share), :] * scale
    out_ref[...] = total
    whole = merge(landed_ref[:, pl.ds(share, landed_ref.shape[1] - share), :])
    rows = whole.shape[0] // 2
    even = jnp.where(core == 0, whole[:rows], whole[rows:])
    odd = jnp.where(core == 0, whole[rows:], whole[:rows])
    lane = lax.broadcasted_iota(jnp.int32, (rows, LANES), 1)
    first = jnp.where(lane < share, even, pltpu.roll(odd, share, 1))
    second = jnp.where(lane < share, pltpu.roll(even, share, 1), odd)
    for k in range(rows):
        for side, values in enumerate((first, second)):
            row = pl.ds(2 * k + side, 1)
            pot_ref[row, :] = base_ref[row, :] - values[k : k + 1]


def rotated(n, first):
    return [(first + place) % n for place in range(n)]


def near_first(n):
    return [n // 2] + sorted(set(range(n)) - {n // 2}, key=lambda place: min(place, n - place))


def scratch(p, q):
    return [
        pltpu.VMEM((p.shape[0], LANES), jnp.float32),
        pltpu.VMEM((p.shape[0], WIDTH), jnp.float32),
        pltpu.VMEM((q.shape[0] // LANES, LANES), jnp.float32),
    ]


def call(kernel, args, outs, scratch_shapes, spaces=None):
    whole = pl.BlockSpec(memory_space=pltpu.VMEM)
    return pl.pallas_call(
        kernel,
        out_shape=outs,
        in_specs=spaces or [whole] * len(args),
        out_specs=jax.tree.map(lambda _: whole, outs),
        scratch_shapes=scratch_shapes,
        compiler_params=pltpu.CompilerParams(vmem_limit_bytes=VMEM_LIMIT),
    )(*args)


def local(source_embed, target_embed, target_feat, source_mass, target_mass):
    f32 = jnp.float32
    shape = jax.ShapeDtypeStruct
    n_src, n_tgt = lax.axis_size("src"), lax.axis_size("tgt")
    rows, depth = source_embed.shape
    width = target_feat.shape[1]
    share, half, chips = rows // n_tgt, rows // 2, n_tgt // 2
    src_mass = source_mass.reshape(-1, LANES)
    tgt_mass = target_mass.reshape(-1, LANES)
    src_rows, tgt_rows = src_mass.shape[0], tgt_mass.shape[0]
    to_src = shape((n_src, tgt_rows, LANES), f32)
    to_tgt = shape((n_tgt, src_rows, LANES), f32)
    by_src = scratch(source_embed, target_embed)
    by_tgt = scratch(target_embed, source_embed)
    far_chip = chips // 2 + math.isqrt(chips) // 2
    same_core = [[2 * chip + core for chip in rotated(chips, far_chip)] for core in range(2)]
    swap = [(index, index ^ 1) for index in range(n_tgt)]

    sems = [pltpu.SemaphoreType.DMA((rows // SLAB,)), pltpu.SemaphoreType.DMA((3,))]
    inputs = [
        pltpu.with_memory_space_constraint(array, pltpu.HBM)
        for array in (source_embed, target_embed, src_mass, tgt_mass)
    ]
    held = [shape(array.shape, array.dtype) for array in inputs]
    sent, source_embed, target_embed, src_log, tgt_log = call(
        first_kernel,
        inputs,
        (to_src, *held),
        sems + by_src,
        [pl.BlockSpec(memory_space=pltpu.HBM)] * len(inputs),
    )
    parts = lax.all_to_all(sent, "src", 0, 0, axis_index_groups=[rotated(n_src, n_src // 2)])
    sent = call(next_kernel, (parts, tgt_log, target_embed, source_embed), to_tgt, by_tgt)
    parts = lax.all_to_all(sent, "tgt", 0, 0, axis_index_groups=[rotated(n_tgt, 2 * far_chip + 1)])
    sent = call(next_kernel, (parts, src_log, source_embed, target_embed), to_src, by_src)
    parts = lax.all_to_all(sent, "src", 0, 0, axis_index_groups=[near_first(n_src)])
    sent, keep, own, bias, turned = call(
        last_kernel,
        (parts, tgt_log, target_embed, source_embed.reshape(chips, 2, share, depth), target_feat),
        (
            shape((width + 8, half), f32),
            shape((target_embed.shape[0], half), jnp.bfloat16),
            shape((8, half), f32),
            shape((tgt_rows, LANES), f32),
            shape(target_feat.shape[::-1], jnp.bfloat16),
        ),
        by_tgt[:2] + by_tgt[1:2],
    )
    came = lax.ppermute(sent, "tgt", swap)
    mean, target_pot, base = call(
        own_kernel,
        (keep, own, turned, bias, target_embed, source_embed, src_log),
        (shape((width, half), f32), shape(bias.shape, f32), shape(src_log.shape, f32)),
        [],
    )
    sent = call(
        functools.partial(pair_kernel, far_chip),
        (mean, own, came),
        shape((chips, share + src_rows, LANES), f32),
        [pltpu.VMEM((src_rows, LANES), f32)],
    )
    landed = lax.all_to_all(sent, "tgt", 0, 0, axis_index_groups=same_core)
    source_pot, projected = call(
        final_kernel,
        (landed, base),
        (shape((src_rows, LANES), f32), shape((share, width), f32)),
        [],
    )
    return (source_pot.reshape(-1), target_pot.reshape(-1), projected)


def solution(mesh):
    placed = (P("src", None), P("tgt", None), P("tgt", None), P("src"), P("tgt"))
    return jax.shard_map(
        local,
        mesh=mesh,
        in_specs=placed,
        out_specs=(P("src"), P("tgt"), P(("src", "tgt"), None)),
        check_vma=False,
    )
```

profile of v0, /device:TPU:1, one launch (start us, length us, event | category | flops | bytes accessed | tf_op | source)
XLA Modules:
  0.0 82.5 jit_solution(5630286078709242752)
XLA Ops:
  0.6 3.1 %shard_map.76 = (f32[16,8,128]{2,1,0:T(8,128)S(1)}, bf16[2048,256]{1,0:T(8,128)(2,1)S(1)}, bf16[1024,256]{1,0:T(8,128)(2,1)S(1)}, f32[16,128]{1,0:T(8,128)S(1)}, f32[8,128]{1,0:T(8,128)S(1)}) custom-call(bf16[2048,256]{1,0:T(8,128)(2,1)} %p_hbm.1, bf16[1024,256]{1,0:T(8,128)(2,1)} %q_hbm.1, f32[16,128]{1,0:T(8,128)} %bitcast.6, f32[8,128]{1,0:T(8,128)} %bitcast.7), custom_call_target="tpu_custom_call" | custom-call | tf_op jit(solution)/shard_map/pallas_call | solution.py:312
  3.8 22.2 %all_to_all.20.parts_ref = f32[16,8,128]{2,1,0:T(8,128)S(1)} all-to-all(f32[16,8,128]{2,1,0:T(8,128)S(1)} %get-tuple-element.18), channel_id=1, replica_groups={{256,288,320,352,384,416,448,480,0,32,64,96,128,160,192,224},{257,289,3..., dimensions={0} | all-to-all | bytes 131072 | tf_op jit(solution)/shard_map/all_to_all | solution.py:353
  25.9 0.0 copy-start
  25.9 1.5 %shard_map.77 = f32[32,16,128]{2,1,0:T(8,128)S(1)} custom-call(f32[16,8,128]{2,1,0:T(8,128)S(1)} %all_to_all.20.parts_ref, f32[8,128]{1,0:T(8,128)S(1)} %get-tuple-element.19.log_ref, bf16[1024,256]{1,0:T(8,128)(2,1)S(1)} %get-tuple-element.20.p_ref.q_ref, bf16[2048,256]{1,0:T(8,128)(2,1)S(1)} %get-tuple-element.21.q_ref.p_ref), custom_call_target="tpu_custom_call" | custom-call | tf_op jit(solution)/shard_map/pallas_call | solution.py:312
  27.5 13.9 %all_to_all.21.parts_ref = f32[32,16,128]{2,1,0:T(8,128)S(1)} all-to-all(f32[32,16,128]{2,1,0:T(8,128)S(1)} %shard_map.77), channel_id=1, replica_groups={{21,22,23,24,25,26,27,28,29,30,31,0,1,2,3,4,5,6,7,8,9,10,11,12,13,14,15..., dimensions={0} | all-to-all | bytes 524288 | tf_op jit(solution)/shard_map/all_to_all | solution.py:355
  41.3 1.6 %shard_map.78 = f32[16,8,128]{2,1,0:T(8,128)S(1)} custom-call(f32[32,16,128]{2,1,0:T(8,128)S(1)} %all_to_all.21.parts_ref, f32[16,128]{1,0:T(8,128)S(1)} %get-tuple-element.22.log_ref, bf16[2048,256]{1,0:T(8,128)(2,1)S(1)} %get-tuple-element.21.q_ref.p_ref, bf16[1024,256]{1,0:T(8,128)(2,1)S(1)} %get-tuple-element.20.p_ref.q_ref), custom_call_target="tpu_custom_call" | custom-call | tf_op jit(solution)/shard_map/pallas_call | solution.py:312
  43.0 14.3 %all_to_all.22.parts_ref = f32[16,8,128]{2,1,0:T(8,128)S(1)} all-to-all(f32[16,8,128]{2,1,0:T(8,128)S(1)} %shard_map.78), channel_id=1, replica_groups={{256,0,32,480,64,448,96,416,128,384,160,352,192,320,224,288},{257,1,33,..., dimensions={0} | all-to-all | bytes 131072 | tf_op jit(solution)/shard_map/all_to_all | solution.py:357
  57.3 0.0 copy-done
  57.3 3.1 %shard_map.79 = (f32[136,1024]{1,0:T(8,128)S(1)}, bf16[1024,1024]{1,0:T(8,128)(2,1)S(1)}, f32[8,1024]{1,0:T(8,128)S(1)}, f32[8,128]{1,0:T(8,128)S(1)}, bf16[128,1024]{1,0:T(8,128)(2,1)S(1)}) custom-call(f32[16,8,128]{2,1,0:T(8,128)S(1)} %all_to_all.22.parts_ref, f32[8,128]{1,0:T(8,128)S(1)} %get-tuple-element.19.log_ref, ...), custom_call_target="tpu_custom_call" | custom-call | tf_op jit(solution)/shard_map/pallas_call | solution.py:312
  60.5 3.7 %collective-permute-start = (f32[136,1024]{1,0:T(8,128)S(1)}, f32[136,1024]{1,0:T(8,128)S(1)}, u32[]{:S(2)}, u32[]{:S(2)}) collective-permute-start(f32[136,1024]{1,0:T(8,128)S(1)} %get-tuple-element.28), channel_id=1, source_target_pairs={{0,1},{1,0},{2,3},{3,2},{4,5},{5,4},{6,7},{7,6},{8,9},{9,8},{10,11... | collective-permute-start | bytes 1671176 | tf_op jit(solution)/shard_map/ppermute | solution.py:370
  64.1 1.4 %shard_map.80 = (f32[128,1024]{1,0:T(8,128)S(1)}, f32[8,128]{1,0:T(8,128)}, f32[16,128]{1,0:T(8,128)S(1)}) custom-call(bf16[1024,1024]{1,0:T(8,128)(2,1)S(1)} %get-tuple-element.23.keep_ref, f32[8,1024]{1,0:T(8,128)S(1)} %get-tuple-element.24.own_ref, bf16[128,1024]{1,0:T(8,128)(2,1)S(1)} %get-tuple-element.25.flip_ref, ...), custom_call_target="tpu_custom_call" | custom-call | tf_op jit(solution)/shard_map/pallas_call | solution.py:312
  65.6 0.1 collective-permute-done.came_ref
  65.7 0.2 shard_map.81
  65.9 15.5 %all_to_all.23.landed_ref = f32[16,80,128]{2,1,0:T(8,128)S(1)} all-to-all(f32[16,80,128]{2,1,0:T(8,128)S(1)} %shard_map.81), channel_id=1, replica_groups={{20,22,24,26,28,30,0,2,4,6,8,10,12,14,16,18},{21,23,25,27,29,31,1,3,5,7..., dimensions={0} | all-to-all | bytes 1310720 | tf_op jit(solution)/shard_map/all_to_all | solution.py:383
  81.4 1.0 %shard_map.82 = (f32[16,128]{1,0:T(8,128)}, f32[64,128]{1,0:T(8,128)}) custom-call(f32[16,80,128]{2,1,0:T(8,128)S(1)} %all_to_all.23.landed_ref, f32[16,128]{1,0:T(8,128)S(1)} %get-tuple-element.29.base_ref), custom_call_target="tpu_custom_call" | custom-call | tf_op jit(solution)/shard_map/pallas_call | solution.py:312
Async XLA Ops:
  25.9 31.4 %copy-start = (bf16[1024,128]{1,0:T(8,128)(2,1)S(1)}, bf16[1024,128]{1,0:T(8,128)(2,1)}, u32[]{:S(2)}) copy-start(bf16[1024,128]{1,0:T(8,128)(2,1)} %feat_ref.1) | copy-start | bytes 786436
  60.5 5.2 %collective-permute-start = (f32[136,1024]{1,0:T(8,128)S(1)}, f32[136,1024]{1,0:T(8,128)S(1)}, u32[]{:S(2)}, u32[]{:S(2)}) collective-permute-start(f32[136,1024]{1,0:T(8,128)S(1)} %get-tuple-element.28), channel_id=1, source_target_pairs={{0,1},{1,0},{2,3},{3,2},{4,5},{5,4},{6,7},{7,6},{8,9},{9,8},{10,11... | collective-permute-start | bytes 1671176 | tf_op jit(solution)/shard_map/ppermute | solution.py:370
where the time goes:
time: 82.8 us; the launch traced here: 82.5 us
  blocking collectives  65.9 us (80%)
  Pallas kernels  12.1 us (15%)
  starting transfers between devices  3.67 us (4%)
    all_to_all x1, blocking collectives, local(): lax.all_to_all(sent, 'src', 0, 0, axis_index_groups=[rotated(n_src, n_src...  22.2 us
    all_to_all x1, blocking collectives, local(): landed = lax.all_to_all(sent, 'tgt', 0, 0, axis_index_groups=same_core)  15.5 us
    all_to_all x1, blocking collectives, local(): lax.all_to_all(sent, 'src', 0, 0, axis_index_groups=[near_first(n_src)])  14.3 us
    all_to_all x1, blocking collectives, local(): lax.all_to_all(sent, 'tgt', 0, 0, axis_index_groups=[rotated(n_tgt, 2 * f...  13.9 us
    pallas_call x7, Pallas kernels, call(): pl.pallas_call(kernel, out_shape=outs, in_specs=spaces or [whole] * len(a...  12.1 us
    ppermute x1, starting transfers between devices, local(): came = lax.ppermute(sent, 'tgt', swap)  3.67 us
  transfers between devices with their start and end apart: 1, of which 1 were waited for; matrix products, arithmetic and copies ran while one was open for 0% of the time, Pallas kernels for 2%

commit v1 on v0

--- a/solution.py
+++ b/solution.py
@@ -78,7 +78,7 @@
     return ONE_UNIT * top + ENTROPY * jnp.log(total)
 
 
-def run_chunks(p_ref, chunk, chunks, col_ref, z_refs, emit, rows=2 * SLAB):
+def run_chunks(p_ref, chunk, chunks, col_ref, z_refs, emit, rows=SLAB):
     slabs = p_ref.shape[0] // rows
     tops = None
     for t in range(chunks + 1):
@@ -295,8 +295,11 @@
     return [(first + place) % n for place in range(n)]
 
 
-def near_first(n):
-    return [n // 2] + sorted(set(range(n)) - {n // 2}, key=lambda place: min(place, n - place))
+def by_distance(n, place):
+    far = n // 2
+    return [far] + sorted(
+        set(range(n)) - {far}, key=lambda other: min((other - place) % n, (place - other) % n)
+    )
 
 
 def scratch(p, q):
@@ -350,11 +353,11 @@
         sems + by_src,
         [pl.BlockSpec(memory_space=pltpu.HBM)] * len(inputs),
     )
-    parts = lax.all_to_all(sent, "src", 0, 0, axis_index_groups=[rotated(n_src, n_src // 2)])
+    parts = lax.all_to_all(sent, "src", 0, 0, axis_index_groups=[by_distance(n_src, n_src // 2)])
     sent = call(next_kernel, (parts, tgt_log, target_embed, source_embed), to_tgt, by_tgt)
     parts = lax.all_to_all(sent, "tgt", 0, 0, axis_index_groups=[rotated(n_tgt, 2 * far_chip + 1)])
     sent = call(next_kernel, (parts, src_log, source_embed, target_embed), to_src, by_src)
-    parts = lax.all_to_all(sent, "src", 0, 0, axis_index_groups=[near_first(n_src)])
+    parts = lax.all_to_all(sent, "src", 0, 0, axis_index_groups=[by_distance(n_src, 0)])
     sent, keep, own, bias, turned = call(
         last_kernel,
         (parts, tgt_log, target_embed, source_embed.reshape(chips, 2, share, depth), target_feat),

time: 82.8 us -> 83.5 us (level)
  no operation moved by 1% of the time
where the time goes in v1:
time: 83.5 us; the launch traced here: 83.2 us
  blocking collectives  66.6 us (80%)
  Pallas kernels  12 us (14%)
  starting transfers between devices  3.78 us (5%)
    all_to_all x1, blocking collectives, local(): lax.all_to_all(sent, 'src', 0, 0, axis_index_groups=[by_distance(n_src, n...  22 us
    all_to_all x1, blocking collectives, local(): landed = lax.all_to_all(sent, 'tgt', 0, 0, axis_index_groups=same_core)  15.6 us
    all_to_all x1, blocking collectives, local(): lax.all_to_all(sent, 'src', 0, 0, axis_index_groups=[by_distance(n_src, 0)])  14.9 us
    all_to_all x1, blocking collectives, local(): lax.all_to_all(sent, 'tgt', 0, 0, axis_index_groups=[rotated(n_tgt, 2 * f...  14 us
    pallas_call x7, Pallas kernels, call(): pl.pallas_call(kernel, out_shape=outs, in_specs=spaces or [whole] * len(a...  12 us
    ppermute x1, starting transfers between devices, local(): came = lax.ppermute(sent, 'tgt', swap)  3.78 us
  transfers between devices with their start and end apart: 1, of which 1 were waited for; matrix products, arithmetic and copies ran while one was open for 0% of the time, Pallas kernels for 2%

profile of v1, /device:TPU:1, one launch (start us, length us, event | category | flops | bytes accessed | tf_op | source)
XLA Modules:
  0.0 83.2 jit_solution(8564008806159194860)
XLA Ops:
  0.6 3.1 %shard_map.76 = (f32[16,8,128]{2,1,0:T(8,128)S(1)}, bf16[2048,256]{1,0:T(8,128)(2,1)S(1)}, bf16[1024,256]{1,0:T(8,128)(2,1)S(1)}, f32[16,128]{1,0:T(8,128)S(1)}, f32[8,128]{1,0:T(8,128)S(1)}) custom-call(bf16[2048,256]{1,0:T(8,128)(2,1)} %p_hbm.1, bf16[1024,256]{1,0:T(8,128)(2,1)} %q_hbm.1, f32[16,128]{1,0:T(8,128)} %bitcast.6, f32[8,128]{1,0:T(8,128)} %bitcast.7), custom_call_target="tpu_custom_call" | custom-call | tf_op jit(solution)/shard_map/pallas_call | solution.py:315
  3.8 22.0 %all_to_all.20.parts_ref = f32[16,8,128]{2,1,0:T(8,128)S(1)} all-to-all(f32[16,8,128]{2,1,0:T(8,128)S(1)} %get-tuple-element.18), channel_id=1, replica_groups={{256,224,288,192,320,160,352,128,384,96,416,64,448,32,480,0},{257,225,2..., dimensions={0} | all-to-all | bytes 131072 | tf_op jit(solution)/shard_map/all_to_all | solution.py:356
  25.8 0.0 copy-start
  25.8 1.5 %shard_map.77 = f32[32,16,128]{2,1,0:T(8,128)S(1)} custom-call(f32[16,8,128]{2,1,0:T(8,128)S(1)} %all_to_all.20.parts_ref, f32[8,128]{1,0:T(8,128)S(1)} %get-tuple-element.19.log_ref, bf16[1024,256]{1,0:T(8,128)(2,1)S(1)} %get-tuple-element.20.p_ref.q_ref, bf16[2048,256]{1,0:T(8,128)(2,1)S(1)} %get-tuple-element.21.q_ref.p_ref), custom_call_target="tpu_custom_call" | custom-call | tf_op jit(solution)/shard_map/pallas_call | solution.py:315
  27.3 14.0 %all_to_all.21.parts_ref = f32[32,16,128]{2,1,0:T(8,128)S(1)} all-to-all(f32[32,16,128]{2,1,0:T(8,128)S(1)} %shard_map.77), channel_id=1, replica_groups={{21,22,23,24,25,26,27,28,29,30,31,0,1,2,3,4,5,6,7,8,9,10,11,12,13,14,15..., dimensions={0} | all-to-all | bytes 524288 | tf_op jit(solution)/shard_map/all_to_all | solution.py:358
  41.3 1.6 %shard_map.78 = f32[16,8,128]{2,1,0:T(8,128)S(1)} custom-call(f32[32,16,128]{2,1,0:T(8,128)S(1)} %all_to_all.21.parts_ref, f32[16,128]{1,0:T(8,128)S(1)} %get-tuple-element.22.log_ref, bf16[2048,256]{1,0:T(8,128)(2,1)S(1)} %get-tuple-element.21.q_ref.p_ref, bf16[1024,256]{1,0:T(8,128)(2,1)S(1)} %get-tuple-element.20.p_ref.q_ref), custom_call_target="tpu_custom_call" | custom-call | tf_op jit(solution)/shard_map/pallas_call | solution.py:315
  43.0 14.9 %all_to_all.22.parts_ref = f32[16,8,128]{2,1,0:T(8,128)S(1)} all-to-all(f32[16,8,128]{2,1,0:T(8,128)S(1)} %shard_map.78), channel_id=1, replica_groups={{256,0,32,480,64,448,96,416,128,384,160,352,192,320,224,288},{257,1,33,..., dimensions={0} | all-to-all | bytes 131072 | tf_op jit(solution)/shard_map/all_to_all | solution.py:360
  57.9 0.0 copy-done
  58.0 3.0 %shard_map.79 = (f32[136,1024]{1,0:T(8,128)S(1)}, bf16[1024,1024]{1,0:T(8,128)(2,1)S(1)}, f32[8,1024]{1,0:T(8,128)S(1)}, f32[8,128]{1,0:T(8,128)S(1)}, bf16[128,1024]{1,0:T(8,128)(2,1)S(1)}) custom-call(f32[16,8,128]{2,1,0:T(8,128)S(1)} %all_to_all.22.parts_ref, f32[8,128]{1,0:T(8,128)S(1)} %get-tuple-element.19.log_ref, ...), custom_call_target="tpu_custom_call" | custom-call | tf_op jit(solution)/shard_map/pallas_call | solution.py:315
  60.9 3.8 %collective-permute-start = (f32[136,1024]{1,0:T(8,128)S(1)}, f32[136,1024]{1,0:T(8,128)S(1)}, u32[]{:S(2)}, u32[]{:S(2)}) collective-permute-start(f32[136,1024]{1,0:T(8,128)S(1)} %get-tuple-element.28), channel_id=1, source_target_pairs={{0,1},{1,0},{2,3},{3,2},{4,5},{5,4},{6,7},{7,6},{8,9},{9,8},{10,11... | collective-permute-start | bytes 1671176 | tf_op jit(solution)/shard_map/ppermute | solution.py:373
  64.7 1.4 %shard_map.80 = (f32[128,1024]{1,0:T(8,128)S(1)}, f32[8,128]{1,0:T(8,128)}, f32[16,128]{1,0:T(8,128)S(1)}) custom-call(bf16[1024,1024]{1,0:T(8,128)(2,1)S(1)} %get-tuple-element.23.keep_ref, f32[8,1024]{1,0:T(8,128)S(1)} %get-tuple-element.24.own_ref, bf16[128,1024]{1,0:T(8,128)(2,1)S(1)} %get-tuple-element.25.flip_ref, ...), custom_call_target="tpu_custom_call" | custom-call | tf_op jit(solution)/shard_map/pallas_call | solution.py:315
  66.2 0.1 collective-permute-done.came_ref
  66.3 0.2 shard_map.81
  66.5 15.6 %all_to_all.23.landed_ref = f32[16,80,128]{2,1,0:T(8,128)S(1)} all-to-all(f32[16,80,128]{2,1,0:T(8,128)S(1)} %shard_map.81), channel_id=1, replica_groups={{20,22,24,26,28,30,0,2,4,6,8,10,12,14,16,18},{21,23,25,27,29,31,1,3,5,7..., dimensions={0} | all-to-all | bytes 1310720 | tf_op jit(solution)/shard_map/all_to_all | solution.py:386
  82.1 1.0 %shard_map.82 = (f32[16,128]{1,0:T(8,128)}, f32[64,128]{1,0:T(8,128)}) custom-call(f32[16,80,128]{2,1,0:T(8,128)S(1)} %all_to_all.23.landed_ref, f32[16,128]{1,0:T(8,128)S(1)} %get-tuple-element.29.base_ref), custom_call_target="tpu_custom_call" | custom-call | tf_op jit(solution)/shard_map/pallas_call | solution.py:315
Async XLA Ops:
  25.8 32.1 %copy-start = (bf16[1024,128]{1,0:T(8,128)(2,1)S(1)}, bf16[1024,128]{1,0:T(8,128)(2,1)}, u32[]{:S(2)}) copy-start(bf16[1024,128]{1,0:T(8,128)(2,1)} %feat_ref.1) | copy-start | bytes 786436
  60.9 5.3 %collective-permute-start = (f32[136,1024]{1,0:T(8,128)S(1)}, f32[136,1024]{1,0:T(8,128)S(1)}, u32[]{:S(2)}, u32[]{:S(2)}) collective-permute-start(f32[136,1024]{1,0:T(8,128)S(1)} %get-tuple-element.28), channel_id=1, source_target_pairs={{0,1},{1,0},{2,3},{3,2},{4,5},{5,4},{6,7},{7,6},{8,9},{9,8},{10,11... | collective-permute-start | bytes 1671176 | tf_op jit(solution)/shard_map/ppermute | solution.py:373

commit v2 on v0

--- a/solution.py
+++ b/solution.py
@@ -78,7 +78,7 @@
     return ONE_UNIT * top + ENTROPY * jnp.log(total)
 
 
-def run_chunks(p_ref, chunk, chunks, col_ref, z_refs, emit, rows=2 * SLAB):
+def run_chunks(p_ref, chunk, chunks, col_ref, z_refs, emit, rows=SLAB):
     slabs = p_ref.shape[0] // rows
     tops = None
     for t in range(chunks + 1):
@@ -97,7 +97,7 @@
             tops = settle(jnp.max, later)
 
 
-def log_sums(p_ref, q_ref, col_ref, z_ref, row_ref, rows=2 * SLAB):
+def log_sums(p_ref, q_ref, col_ref, z_ref, row_ref, out_ref, rows=2 * SLAB):
     slabs, chunks = p_ref.shape[0] // SLAB, q_ref.shape[0] // WIDTH
     totals = [None] * chunks
     for s in range(p_ref.shape[0] // rows):
@@ -108,7 +108,7 @@
         for h, total in enumerate(settle(jnp.sum, totals[t])):
             row_ref[pl.ds(t * HALVES + h, 1), :] = total
     sums = row_ref[...]
-    row_ref[...] = ENTROPY * jnp.log(sums)
+    out_ref[...] = jnp.broadcast_to((ENTROPY * jnp.log(sums))[None], out_ref.shape)
     safe = jnp.logical_and(jnp.min(sums) >= LOWEST, jnp.max(sums) <= HIGHEST)
 
     @pl.when(jnp.logical_not(safe))
@@ -124,6 +124,8 @@
                 sums = join(jnp.add, sums, weigh(z_ref, tops, s)[1])
             for h, pair in enumerate(zip(tops, settle(jnp.sum, sums))):
                 row_ref[pl.ds(t * HALVES + h, 1), :] = log_sum(*pair)
+
+        out_ref[...] = jnp.broadcast_to(row_ref[...][None], out_ref.shape)
 
 
 def first_kernel(
@@ -147,19 +149,16 @@
         p = p_ref[slab, :].astype(jnp.float32)
         norms = jnp.sum(p * p, axis=1, keepdims=True)
         col_ref[slab, :] = jnp.broadcast_to(-ONE_SCALE * norms, (SLAB, LANES))
-    load_q.wait()
-    log_sums(p_ref, q_ref, col_ref, z_ref, row_ref)
-    for copy in masses:
+    for copy in masses + [load_q]:
         copy.wait()
     p_log_ref[...] = ENTROPY * jnp.log(p_log_ref[...])
     q_log_ref[...] = ENTROPY * jnp.log(q_log_ref[...])
-    out_ref[...] = jnp.broadcast_to(row_ref[...][None], out_ref.shape)
+    log_sums(p_ref, q_ref, col_ref, z_ref, row_ref, out_ref)
 
 
 def next_kernel(parts_ref, log_ref, p_ref, q_ref, out_ref, col_ref, z_ref, row_ref):
     lanes_to_rows(ONE_SCALE * (log_ref[...] - merge(parts_ref[...])), col_ref)
-    log_sums(p_ref, q_ref, col_ref, z_ref, row_ref)
-    out_ref[...] = jnp.broadcast_to(row_ref[...][None], out_ref.shape)
+    log_sums(p_ref, q_ref, col_ref, z_ref, row_ref, out_ref)
 
 
 def last_kernel(

time: 82.8 us -> 82.5 us (level)
  no operation moved by 1% of the time
where the time goes in v2:
time: 82.5 us; the launch traced here: 82.3 us
  blocking collectives  65.8 us (80%)
  Pallas kernels  11.9 us (14%)
  starting transfers between devices  3.68 us (4%)
    all_to_all x1, blocking collectives, local(): lax.all_to_all(sent, 'src', 0, 0, axis_index_groups=[rotated(n_src, n_src...  22.2 us
    all_to_all x1, blocking collectives, local(): landed = lax.all_to_all(sent, 'tgt', 0, 0, axis_index_groups=same_core)  15.5 us
    all_to_all x1, blocking collectives, local(): lax.all_to_all(sent, 'src', 0, 0, axis_index_groups=[near_first(n_src)])  14.3 us
    all_to_all x1, blocking collectives, local(): lax.all_to_all(sent, 'tgt', 0, 0, axis_index_groups=[rotated(n_tgt, 2 * f...  13.9 us
    pallas_call x7, Pallas kernels, call(): pl.pallas_call(kernel, out_shape=outs, in_specs=spaces or [whole] * len(a...  11.9 us
    ppermute x1, starting transfers between devices, local(): came = lax.ppermute(sent, 'tgt', swap)  3.68 us
  transfers between devices with their start and end apart: 1, of which 1 were waited for; matrix products, arithmetic and copies ran while one was open for 0% of the time, Pallas kernels for 2%

profile of v2, /device:TPU:1, one launch (start us, length us, event | category | flops | bytes accessed | tf_op | source)
XLA Modules:
  0.0 82.3 jit_solution(5002167726785192744)
XLA Ops:
  0.6 3.1 %shard_map.76 = (f32[16,8,128]{2,1,0:T(8,128)S(1)}, bf16[2048,256]{1,0:T(8,128)(2,1)S(1)}, bf16[1024,256]{1,0:T(8,128)(2,1)S(1)}, f32[16,128]{1,0:T(8,128)S(1)}, f32[8,128]{1,0:T(8,128)S(1)}) custom-call(bf16[2048,256]{1,0:T(8,128)(2,1)} %p_hbm.1, bf16[1024,256]{1,0:T(8,128)(2,1)} %q_hbm.1, f32[16,128]{1,0:T(8,128)} %bitcast.6, f32[8,128]{1,0:T(8,128)} %bitcast.7), custom_call_target="tpu_custom_call" | custom-call | tf_op jit(solution)/shard_map/pallas_call | solution.py:311
  3.8 22.2 %all_to_all.20.parts_ref = f32[16,8,128]{2,1,0:T(8,128)S(1)} all-to-all(f32[16,8,128]{2,1,0:T(8,128)S(1)} %get-tuple-element.18), channel_id=1, replica_groups={{256,288,320,352,384,416,448,480,0,32,64,96,128,160,192,224},{257,289,3..., dimensions={0} | all-to-all | bytes 131072 | tf_op jit(solution)/shard_map/all_to_all | solution.py:352
  25.9 0.0 copy-start
  25.9 1.5 %shard_map.77 = f32[32,16,128]{2,1,0:T(8,128)S(1)} custom-call(f32[16,8,128]{2,1,0:T(8,128)S(1)} %all_to_all.20.parts_ref, f32[8,128]{1,0:T(8,128)S(1)} %get-tuple-element.19.log_ref, bf16[1024,256]{1,0:T(8,128)(2,1)S(1)} %get-tuple-element.20.p_ref.q_ref, bf16[2048,256]{1,0:T(8,128)(2,1)S(1)} %get-tuple-element.21.q_ref.p_ref), custom_call_target="tpu_custom_call" | custom-call | tf_op jit(solution)/shard_map/pallas_call | solution.py:311
  27.4 13.9 %all_to_all.21.parts_ref = f32[32,16,128]{2,1,0:T(8,128)S(1)} all-to-all(f32[32,16,128]{2,1,0:T(8,128)S(1)} %shard_map.77), channel_id=1, replica_groups={{21,22,23,24,25,26,27,28,29,30,31,0,1,2,3,4,5,6,7,8,9,10,11,12,13,14,15..., dimensions={0} | all-to-all | bytes 524288 | tf_op jit(solution)/shard_map/all_to_all | solution.py:354
  41.3 1.6 %shard_map.78 = f32[16,8,128]{2,1,0:T(8,128)S(1)} custom-call(f32[32,16,128]{2,1,0:T(8,128)S(1)} %all_to_all.21.parts_ref, f32[16,128]{1,0:T(8,128)S(1)} %get-tuple-element.22.log_ref, bf16[2048,256]{1,0:T(8,128)(2,1)S(1)} %get-tuple-element.21.q_ref.p_ref, bf16[1024,256]{1,0:T(8,128)(2,1)S(1)} %get-tuple-element.20.p_ref.q_ref), custom_call_target="tpu_custom_call" | custom-call | tf_op jit(solution)/shard_map/pallas_call | solution.py:311
  43.0 14.3 %all_to_all.22.parts_ref = f32[16,8,128]{2,1,0:T(8,128)S(1)} all-to-all(f32[16,8,128]{2,1,0:T(8,128)S(1)} %shard_map.78), channel_id=1, replica_groups={{256,0,32,480,64,448,96,416,128,384,160,352,192,320,224,288},{257,1,33,..., dimensions={0} | all-to-all | bytes 131072 | tf_op jit(solution)/shard_map/all_to_all | solution.py:356
  57.3 0.0 copy-done
  57.3 3.0 %shard_map.79 = (f32[136,1024]{1,0:T(8,128)S(1)}, bf16[1024,1024]{1,0:T(8,128)(2,1)S(1)}, f32[8,1024]{1,0:T(8,128)S(1)}, f32[8,128]{1,0:T(8,128)S(1)}, bf16[128,1024]{1,0:T(8,128)(2,1)S(1)}) custom-call(f32[16,8,128]{2,1,0:T(8,128)S(1)} %all_to_all.22.parts_ref, f32[8,128]{1,0:T(8,128)S(1)} %get-tuple-element.19.log_ref, ...), custom_call_target="tpu_custom_call" | custom-call | tf_op jit(solution)/shard_map/pallas_call | solution.py:311
  60.3 3.7 %collective-permute-start = (f32[136,1024]{1,0:T(8,128)S(1)}, f32[136,1024]{1,0:T(8,128)S(1)}, u32[]{:S(2)}, u32[]{:S(2)}) collective-permute-start(f32[136,1024]{1,0:T(8,128)S(1)} %get-tuple-element.28), channel_id=1, source_target_pairs={{0,1},{1,0},{2,3},{3,2},{4,5},{5,4},{6,7},{7,6},{8,9},{9,8},{10,11... | collective-permute-start | bytes 1671176 | tf_op jit(solution)/shard_map/ppermute | solution.py:369
  63.9 1.4 %shard_map.80 = (f32[128,1024]{1,0:T(8,128)S(1)}, f32[8,128]{1,0:T(8,128)}, f32[16,128]{1,0:T(8,128)S(1)}) custom-call(bf16[1024,1024]{1,0:T(8,128)(2,1)S(1)} %get-tuple-element.23.keep_ref, f32[8,1024]{1,0:T(8,128)S(1)} %get-tuple-element.24.own_ref, bf16[128,1024]{1,0:T(8,128)(2,1)S(1)} %get-tuple-element.25.flip_ref, ...), custom_call_target="tpu_custom_call" | custom-call | tf_op jit(solution)/shard_map/pallas_call | solution.py:311
  65.4 0.1 collective-permute-done.came_ref
  65.5 0.2 shard_map.81
  65.7 15.5 %all_to_all.23.landed_ref = f32[16,80,128]{2,1,0:T(8,128)S(1)} all-to-all(f32[16,80,128]{2,1,0:T(8,128)S(1)} %shard_map.81), channel_id=1, replica_groups={{20,22,24,26,28,30,0,2,4,6,8,10,12,14,16,18},{21,23,25,27,29,31,1,3,5,7..., dimensions={0} | all-to-all | bytes 1310720 | tf_op jit(solution)/shard_map/all_to_all | solution.py:382
  81.2 1.0 %shard_map.82 = (f32[16,128]{1,0:T(8,128)}, f32[64,128]{1,0:T(8,128)}) custom-call(f32[16,80,128]{2,1,0:T(8,128)S(1)} %all_to_all.23.landed_ref, f32[16,128]{1,0:T(8,128)S(1)} %get-tuple-element.29.base_ref), custom_call_target="tpu_custom_call" | custom-call | tf_op jit(solution)/shard_map/pallas_call | solution.py:311
Async XLA Ops:
  25.9 31.3 %copy-start = (bf16[1024,128]{1,0:T(8,128)(2,1)S(1)}, bf16[1024,128]{1,0:T(8,128)(2,1)}, u32[]{:S(2)}) copy-start(bf16[1024,128]{1,0:T(8,128)(2,1)} %feat_ref.1) | copy-start | bytes 786436
  60.3 5.3 %collective-permute-start = (f32[136,1024]{1,0:T(8,128)S(1)}, f32[136,1024]{1,0:T(8,128)S(1)}, u32[]{:S(2)}, u32[]{:S(2)}) collective-permute-start(f32[136,1024]{1,0:T(8,128)S(1)} %get-tuple-element.28), channel_id=1, source_target_pairs={{0,1},{1,0},{2,3},{3,2},{4,5},{5,4},{6,7},{7,6},{8,9},{9,8},{10,11... | collective-permute-start | bytes 1671176 | tf_op jit(solution)/shard_map/ppermute | solution.py:369

commit v3 on v2

--- a/solution.py
+++ b/solution.py
@@ -10,7 +10,7 @@
 
 ENTROPY = 0.05
 LANES = 128
-WIDTH = 256
+WIDTH = 512
 ONE_SCALE = 1.0 / ENTROPY * math.log2(math.e)
 TWO_SCALE = 2.0 * ONE_SCALE
 ONE_UNIT = ENTROPY * math.log(2.0)

time: 82.5 us -> 82.8 us (level)
  no operation moved by 1% of the time
where the time goes in v3:
time: 82.8 us; the launch traced here: 82.6 us
  blocking collectives  65.7 us (79%)
  Pallas kernels  12.1 us (15%)
  starting transfers between devices  3.92 us (5%)
    all_to_all x1, blocking collectives, local(): lax.all_to_all(sent, 'src', 0, 0, axis_index_groups=[rotated(n_src, n_src...  22.2 us
    all_to_all x1, blocking collectives, local(): landed = lax.all_to_all(sent, 'tgt', 0, 0, axis_index_groups=same_core)  15.5 us
    all_to_all x1, blocking collectives, local(): lax.all_to_all(sent, 'src', 0, 0, axis_index_groups=[near_first(n_src)])  14.1 us
    all_to_all x1, blocking collectives, local(): lax.all_to_all(sent, 'tgt', 0, 0, axis_index_groups=[rotated(n_tgt, 2 * f...  13.9 us
    pallas_call x7, Pallas kernels, call(): pl.pallas_call(kernel, out_shape=outs, in_specs=spaces or [whole] * len(a...  12.1 us
    ppermute x1, starting transfers between devices, local(): came = lax.ppermute(sent, 'tgt', swap)  3.92 us
  transfers between devices with their start and end apart: 1, of which 1 were waited for; matrix products, arithmetic and copies ran while one was open for 0% of the time, Pallas kernels for 2%

profile of v3, /device:TPU:1, one launch (start us, length us, event | category | flops | bytes accessed | tf_op | source)
XLA Modules:
  0.0 82.6 jit_solution(1203352272371569470)
XLA Ops:
  0.6 3.1 %shard_map.76 = (f32[16,8,128]{2,1,0:T(8,128)S(1)}, bf16[2048,256]{1,0:T(8,128)(2,1)S(1)}, bf16[1024,256]{1,0:T(8,128)(2,1)S(1)}, f32[16,128]{1,0:T(8,128)S(1)}, f32[8,128]{1,0:T(8,128)S(1)}) custom-call(bf16[2048,256]{1,0:T(8,128)(2,1)} %p_hbm.1, bf16[1024,256]{1,0:T(8,128)(2,1)} %q_hbm.1, f32[16,128]{1,0:T(8,128)} %bitcast.6, f32[8,128]{1,0:T(8,128)} %bitcast.7), custom_call_target="tpu_custom_call" | custom-call | tf_op jit(solution)/shard_map/pallas_call | solution.py:311
  3.8 22.2 %all_to_all.20.parts_ref = f32[16,8,128]{2,1,0:T(8,128)S(1)} all-to-all(f32[16,8,128]{2,1,0:T(8,128)S(1)} %get-tuple-element.18), channel_id=1, replica_groups={{256,288,320,352,384,416,448,480,0,32,64,96,128,160,192,224},{257,289,3..., dimensions={0} | all-to-all | bytes 131072 | tf_op jit(solution)/shard_map/all_to_all | solution.py:352
  25.9 0.0 copy-start
  25.9 1.5 %shard_map.77 = f32[32,16,128]{2,1,0:T(8,128)S(1)} custom-call(f32[16,8,128]{2,1,0:T(8,128)S(1)} %all_to_all.20.parts_ref, f32[8,128]{1,0:T(8,128)S(1)} %get-tuple-element.19.log_ref, bf16[1024,256]{1,0:T(8,128)(2,1)S(1)} %get-tuple-element.20.p_ref.q_ref, bf16[2048,256]{1,0:T(8,128)(2,1)S(1)} %get-tuple-element.21.q_ref.p_ref), custom_call_target="tpu_custom_call" | custom-call | tf_op jit(solution)/shard_map/pallas_call | solution.py:311
  27.4 13.9 %all_to_all.21.parts_ref = f32[32,16,128]{2,1,0:T(8,128)S(1)} all-to-all(f32[32,16,128]{2,1,0:T(8,128)S(1)} %shard_map.77), channel_id=1, replica_groups={{21,22,23,24,25,26,27,28,29,30,31,0,1,2,3,4,5,6,7,8,9,10,11,12,13,14,15..., dimensions={0} | all-to-all | bytes 524288 | tf_op jit(solution)/shard_map/all_to_all | solution.py:354
  41.3 1.6 %shard_map.78 = f32[16,8,128]{2,1,0:T(8,128)S(1)} custom-call(f32[32,16,128]{2,1,0:T(8,128)S(1)} %all_to_all.21.parts_ref, f32[16,128]{1,0:T(8,128)S(1)} %get-tuple-element.22.log_ref, bf16[2048,256]{1,0:T(8,128)(2,1)S(1)} %get-tuple-element.21.q_ref.p_ref, bf16[1024,256]{1,0:T(8,128)(2,1)S(1)} %get-tuple-element.20.p_ref.q_ref), custom_call_target="tpu_custom_call" | custom-call | tf_op jit(solution)/shard_map/pallas_call | solution.py:311
  43.0 14.1 %all_to_all.22.parts_ref = f32[16,8,128]{2,1,0:T(8,128)S(1)} all-to-all(f32[16,8,128]{2,1,0:T(8,128)S(1)} %shard_map.78), channel_id=1, replica_groups={{256,0,32,480,64,448,96,416,128,384,160,352,192,320,224,288},{257,1,33,..., dimensions={0} | all-to-all | bytes 131072 | tf_op jit(solution)/shard_map/all_to_all | solution.py:356
  57.1 0.0 copy-done
  57.1 3.2 %shard_map.79 = (f32[136,1024]{1,0:T(8,128)S(1)}, bf16[1024,1024]{1,0:T(8,128)(2,1)S(1)}, f32[8,1024]{1,0:T(8,128)S(1)}, f32[8,128]{1,0:T(8,128)S(1)}, bf16[128,1024]{1,0:T(8,128)(2,1)S(1)}) custom-call(f32[16,8,128]{2,1,0:T(8,128)S(1)} %all_to_all.22.parts_ref, f32[8,128]{1,0:T(8,128)S(1)} %get-tuple-element.19.log_ref, ...), custom_call_target="tpu_custom_call" | custom-call | tf_op jit(solution)/shard_map/pallas_call | solution.py:311
  60.3 3.9 %collective-permute-start = (f32[136,1024]{1,0:T(8,128)S(1)}, f32[136,1024]{1,0:T(8,128)S(1)}, u32[]{:S(2)}, u32[]{:S(2)}) collective-permute-start(f32[136,1024]{1,0:T(8,128)S(1)} %get-tuple-element.28), channel_id=1, source_target_pairs={{0,1},{1,0},{2,3},{3,2},{4,5},{5,4},{6,7},{7,6},{8,9},{9,8},{10,11... | collective-permute-start | bytes 1671176 | tf_op jit(solution)/shard_map/ppermute | solution.py:369
  64.2 1.4 %shard_map.80 = (f32[128,1024]{1,0:T(8,128)S(1)}, f32[8,128]{1,0:T(8,128)}, f32[16,128]{1,0:T(8,128)S(1)}) custom-call(bf16[1024,1024]{1,0:T(8,128)(2,1)S(1)} %get-tuple-element.23.keep_ref, f32[8,1024]{1,0:T(8,128)S(1)} %get-tuple-element.24.own_ref, bf16[128,1024]{1,0:T(8,128)(2,1)S(1)} %get-tuple-element.25.flip_ref, ...), custom_call_target="tpu_custom_call" | custom-call | tf_op jit(solution)/shard_map/pallas_call | solution.py:311
  65.7 0.1 collective-permute-done.came_ref
  65.8 0.2 shard_map.81
  66.0 15.5 %all_to_all.23.landed_ref = f32[16,80,128]{2,1,0:T(8,128)S(1)} all-to-all(f32[16,80,128]{2,1,0:T(8,128)S(1)} %shard_map.81), channel_id=1, replica_groups={{20,22,24,26,28,30,0,2,4,6,8,10,12,14,16,18},{21,23,25,27,29,31,1,3,5,7..., dimensions={0} | all-to-all | bytes 1310720 | tf_op jit(solution)/shard_map/all_to_all | solution.py:382
  81.5 1.0 %shard_map.82 = (f32[16,128]{1,0:T(8,128)}, f32[64,128]{1,0:T(8,128)}) custom-call(f32[16,80,128]{2,1,0:T(8,128)S(1)} %all_to_all.23.landed_ref, f32[16,128]{1,0:T(8,128)S(1)} %get-tuple-element.29.base_ref), custom_call_target="tpu_custom_call" | custom-call | tf_op jit(solution)/shard_map/pallas_call | solution.py:311
Async XLA Ops:
  25.9 31.2 %copy-start = (bf16[1024,128]{1,0:T(8,128)(2,1)S(1)}, bf16[1024,128]{1,0:T(8,128)(2,1)}, u32[]{:S(2)}) copy-start(bf16[1024,128]{1,0:T(8,128)(2,1)} %feat_ref.1) | copy-start | bytes 786436
  60.3 5.5 %collective-permute-start = (f32[136,1024]{1,0:T(8,128)S(1)}, f32[136,1024]{1,0:T(8,128)S(1)}, u32[]{:S(2)}, u32[]{:S(2)}) collective-permute-start(f32[136,1024]{1,0:T(8,128)S(1)} %get-tuple-element.28), channel_id=1, source_target_pairs={{0,1},{1,0},{2,3},{3,2},{4,5},{5,4},{6,7},{7,6},{8,9},{9,8},{10,11... | collective-permute-start | bytes 1671176 | tf_op jit(solution)/shard_map/ppermute | solution.py:369
